TPU v7x, 128 devices: a whole 4x4x4 slice. The times are simulated.
128 devices in a mesh: dp: 8 (over y, core), mp: 16 (over z, x).
Axes of the slice: x: 4, y: 4, z: 4, core: 2. Of those that a mesh axis runs over, the one named last changes fastest.
Arguments:
- saved_acts: bfloat16 [6144, 18432], P('dp', 'mp'), may hold values from -6 to 6
- solution: float32 [18432, 4608], P('mp', 'dp'), may hold values from -6 to 6
- residual: float32 [18432, 4608], P('mp', 'dp'), may hold values from -6 to 6
- direction: float32 [18432, 4608], P('mp', 'dp'), may hold values from -6 to 6
Outputs:
- new_solution: float32 [18432, 4608], P('mp', 'dp')
- new_residual: float32 [18432, 4608], P('mp', 'dp')
- new_direction: float32 [18432, 4608], P('mp', 'dp')
All inputs are finite; a program needn't handle non-finite values.
Results may differ from a plain program's by a relative error of at most 0.0029.
Values may be sent and summed in bfloat16 or wider, within the bound.
A program may use at most 128 MiB of HBM per device.

v0:
```python
import jax
import jax.numpy as jnp
from jax import lax
from jax.sharding import PartitionSpec as P


def total_tangent(partial_tan):
    return lax.psum(partial_tan, "mp").astype(jnp.bfloat16)


def body(saved_acts, solution, residual, direction):
    low_dir = direction.astype(jnp.bfloat16)
    partial_tan = jnp.dot(
        saved_acts,
        lax.all_gather(low_dir, "dp", axis=1, tiled=True),
        preferred_element_type=jnp.float32,
    )
    tangent = total_tangent(partial_tan)
    partial_back = lax.dot_general(
        saved_acts, tangent, (((0,), (0,)), ((), ())), preferred_element_type=jnp.float32
    )
    pulled = lax.psum_scatter(partial_back, "dp", scatter_dimension=1, tiled=True)
    total_tokens = saved_acts.shape[0] * lax.axis_size("dp")
    curved = pulled / total_tokens + 1.0 * direction
    norm_old, along = lax.psum(
        (jnp.sum(residual * residual), jnp.sum(direction * curved)), ("dp", "mp")
    )
    step_size = norm_old / along
    new_residual = residual - step_size * curved
    norm_new = lax.psum(jnp.sum(new_residual * new_residual), ("dp", "mp"))
    new_solution = solution + step_size * direction
    new_direction = new_residual + norm_new / norm_old * direction
    return (new_solution, new_residual, new_direction)


def solution(mesh):
    return jax.shard_map(
        body,
        mesh=mesh,
        in_specs=(P("dp", "mp"), P("mp", "dp"), P("mp", "dp"), P("mp", "dp")),
        out_specs=(P("mp", "dp"), P("mp", "dp"), P("mp", "dp")),
        check_vma=False,
    )
```

profile of v0, /device:TPU:1, one launch (start us, length us, event | category | flops | bytes accessed | tf_op | source)
XLA Modules:
  0.0 679.2 jit_solution(6731292511349068798)
XLA Ops:
  7.2 0.0 copy-start
  7.2 0.0 all-gather.2.cloned.1.call-start
  7.2 3.1 convert_element_type.6
  10.3 0.0 all-gather.2.cloned.1.call-update
  10.3 0.0 reduce-scatter.2.cloned.1.call-start
  10.4 62.8 %all-gather.2.cloned.1.call-done = bf16[1152,4608]{0,1:T(8,128)(2,1)} async-done(((bf16[1152,576]{0,1:T(8,128)(2,1)}), bf16[1152,4608]{0,1:T(8,128)(2,1)}) %all-gather.2.cloned.1.call-update) | async-done | bytes 10616848 | tf_op jit(solution)/shard_map/all_gather | solution.py:15
  73.2 0.0 copy-done
  73.2 14.9 %fusion.1 = f32[768,4608]{1,0:T(8,128)} fusion(bf16[768,1152]{1,0:T(8,128)(2,1)S(1)} %copy-done, bf16[1152,4608]{0,1:T(8,128)(2,1)} %all-gather.2.cloned.1.call-done), kind=kOutput, calls=%fused_computation.9 | convolution fusion | flops 8153726976 | bytes 26542080 | tf_op jit(solution)/shard_map/dot_general | solution.py:13
  88.1 308.5 %all-reduce.2 = bf16[768,4608]{1,0:T(8,128)(2,1)} all-reduce(f32[768,4608]{1,0:T(8,128)} %fusion.1), channel_id=1, replica_groups=mesh['dp'=8,'mp'=16] {'mp'}, use_global_device_ids=true, to_apply=%region_2.0 | all-reduce | flops 3538944 | bytes 21233664 | tf_op jit(solution)/shard_map/psum | solution.py:8
  396.6 15.5 %convolution_bitcast_fusion = f32[1152,4608]{0,1:T(8,128)} fusion(bf16[768,1152]{1,0:T(8,128)(2,1)S(1)} %copy-done, bf16[768,4608]{1,0:T(8,128)(2,1)} %all-reduce.2), kind=kOutput, calls=%fused_computation | convolution fusion | flops 8153726976 | bytes 30081024 | tf_op jit(solution)/shard_map/dot_general | solution.py:19
  412.1 0.0 reduce-scatter.2.cloned.1.call-update
  412.1 3.0 multiply_reduce_fusion.2
  415.2 109.1 %reduce-scatter.2.cloned.1.call-done = f32[1152,576]{0,1:T(8,128)} async-done(((f32[1152,4608]{0,1:T(8,128)}), f32[1152,576]{0,1:T(8,128)}) %reduce-scatter.2.cloned.1.call-update) | async-done | bytes 2654224 | tf_op jit(solution)/shard_map/reduce_scatter | solution.py:22
  524.2 3.8 multiply_reduce_fusion.1
  528.1 65.4 %all-reduce = (f32[]{:T(128)}, f32[]{:T(128)}) all-reduce(f32[]{:T(128)} %multiply_reduce_fusion.2, f32[]{:T(128)} %multiply_reduce_fusion.1), channel_id=1, replica_groups=mesh['dp'=8,'mp'=16] {'dp','mp'}, use_global_device_ids=true, to_apply=%region_1.0 | all-reduce | flops 2 | bytes 16 | tf_op jit(solution)/shard_map/psum | solution.py:25
  594.9 6.1 multiply_reduce_fusion
  600.9 63.9 %psum.31 = f32[]{:T(128)} all-reduce(f32[]{:T(128)} %get-tuple-element.5), channel_id=1, replica_groups=mesh['dp'=8,'mp'=16] {'dp','mp'}, use_global_device_ids=true, to_apply=%region_7.0 | all-reduce | flops 1 | bytes 8 | tf_op jit(solution)/shard_map/psum | solution.py:30
  666.1 0.0 copy-start.1
  666.1 6.3 multiply_add_fusion
  672.4 0.0 copy-done.1
Async XLA Ops:
  7.2 66.0 %copy-start = (bf16[768,1152]{1,0:T(8,128)(2,1)S(1)}, bf16[768,1152]{1,0:T(8,128)(2,1)}, u32[]{:S(2)}) copy-start(bf16[768,1152]{1,0:T(8,128)(2,1)} %param.4) | copy-start | bytes 5308420
  7.2 66.0 %all-gather.2.cloned.1.call-start = ((), (), s32[]{:S(2)}) async-start(), calls=%async_computation.1 | async-start | bytes 11943936 | tf_op jit(solution)/shard_map/all_gather | solution.py:15
  10.3 513.9 %reduce-scatter.2.cloned.1.call-start = ((), (), s32[]{:S(2)}) async-start(), calls=%async_computation.2 | async-start | bytes 23887872 | tf_op jit(solution)/shard_map/reduce_scatter | solution.py:22
  666.1 6.3 copy-start.1
Sparse Core Ops, SparseCore 0:
  10.4 62.7 all-gather.1
  412.2 111.9 reduce-scatter.1
where the time goes:
time: 680 us; the launch traced here: 679 us
  blocking collectives  438 us (64%)
  waiting for transfers between devices  172 us (25%)
  matrix products  30.4 us (4%)
  other arithmetic  22.3 us (3%)
  between operations  16.7 us (2%)
    psum x1, blocking collectives, total_tangent(): return lax.psum(partial_tan, 'mp').astype(jnp.bfloat16)  308 us
    reduce_scatter x1, waiting for transfers between devices, body(): lax.psum_scatter(partial_back, 'dp', scatter_dimension=1, tiled=True)  109 us
    psum x1, blocking collectives, body(): lax.psum((jnp.sum(residual * residual), jnp.sum(direction * curved)), ('d...  65.4 us
    psum x1, blocking collectives, body(): norm_new = lax.psum(jnp.sum(new_residual * new_residual), ('dp', 'mp'))  63.9 us
    all_gather x1, waiting for transfers between devices, body(): lax.all_gather(low_dir, 'dp', axis=1, tiled=True)  62.8 us
    dot_general x1, matrix products, body(): lax.dot_general(saved_acts, tangent, (((0,), (0,)), ((), ())), preferred_...  15.5 us
    dot_general x1, matrix products, body(): jnp.dot(saved_acts, lax.all_gather(low_dir, 'dp', axis=1, tiled=True), pr...  14.9 us
  transfers between devices with their start and end apart: 2, of which 2 were waited for; matrix products, arithmetic and copies ran while one was open for 0% of the time, Pallas kernels for 0%

commit v1 on v0

v1 whole, which is shorter than its diff:
```python
import jax
import jax.numpy as jnp
from jax import lax
from jax.sharding import PartitionSpec as P


def body(saved_acts, solution, residual, direction):
    low_dir = direction.astype(jnp.bfloat16)
    acts = lax.all_gather(saved_acts, "dp", axis=0, tiled=True)
    partial_tan = jnp.dot(acts, low_dir, preferred_element_type=jnp.float32)
    mine = lax.psum_scatter(partial_tan, "mp", scatter_dimension=0, tiled=True)
    tangent = lax.all_gather(mine.astype(jnp.bfloat16), "mp", axis=0, tiled=True)
    pulled = lax.dot_general(
        acts, tangent, (((0,), (0,)), ((), ())), preferred_element_type=jnp.float32
    )
    curved = pulled / acts.shape[0] + 1.0 * direction
    sums = jnp.stack(
        [
            jnp.sum(residual * residual),
            jnp.sum(direction * curved),
            jnp.sum(residual * curved),
            jnp.sum(curved * curved),
        ]
    )
    norm_old, along, res_curved, curved_sq = lax.psum(sums, ("dp", "mp"))
    step_size = norm_old / along
    new_residual = residual - step_size * curved
    norm_new = norm_old + step_size * (step_size * curved_sq - 2.0 * res_curved)
    new_solution = solution + step_size * direction
    new_direction = new_residual + norm_new / norm_old * direction
    return (new_solution, new_residual, new_direction)


def solution(mesh):
    return jax.shard_map(
        body,
        mesh=mesh,
        in_specs=(P("dp", "mp"), P("mp", "dp"), P("mp", "dp"), P("mp", "dp")),
        out_specs=(P("mp", "dp"), P("mp", "dp"), P("mp", "dp")),
        check_vma=False,
    )
```

time: 680 us -> 380 us (0.56)
  blocking collectives: 438 us -> 65.1 us
  waiting for transfers between devices: 172 us -> 251 us
  other arithmetic: 22.3 us -> 11.6 us
    psum x3 -> x1, blocking collectives: 438 us -> 65.1 us  [body(): norm_old, along, res_curved, curved_sq = lax.psum(sums, ('dp', 'mp'))]
    all_gather x1 -> x2, waiting for transfers between devices: 62.8 us -> 150 us  [the longest x1 79.4 us: body(): acts = lax.all_gather(saved_acts, 'dp', axis=0, tiled=True)]
    reduce_sum x3 -> x0, other arithmetic: 12.9 us -> none  [the longest x1 6.06 us: body(): norm_new = lax.psum(jnp.sum(new_residual * new_residual), ('dp', 'mp'))]
    reduce_scatter x1, waiting for transfers between devices: 109 us -> 99.8 us  [body(): mine = lax.psum_scatter(partial_tan, 'mp', scatter_dimension=0, tiled=True)]
  transfers between devices with their start and end apart: 2 -> 3, of which waited for: 2 -> 3; matrix products, arithmetic and copies ran while one was open for 0% -> 0% of each run, Pallas kernels for 0% -> 0%
where the time goes in v1:
time: 380 us; the launch traced here: 379 us
  waiting for transfers between devices  251 us (66%)
  blocking collectives  65.1 us (17%)
  matrix products  33.5 us (9%)
  between operations  17.5 us (5%)
  other arithmetic  11.6 us (3%)
    reduce_scatter x1, waiting for transfers between devices, body(): mine = lax.psum_scatter(partial_tan, 'mp', scatter_dimension=0, tiled=True)  99.8 us
    all_gather x1, waiting for transfers between devices, body(): acts = lax.all_gather(saved_acts, 'dp', axis=0, tiled=True)  79.4 us
    all_gather x1, waiting for transfers between devices, body(): lax.all_gather(mine.astype(jnp.bfloat16), 'mp', axis=0, tiled=True)  70.8 us
    psum x1, blocking collectives, body(): norm_old, along, res_curved, curved_sq = lax.psum(sums, ('dp', 'mp'))  65.1 us
    dot_general x1, matrix products, body(): lax.dot_general(acts, tangent, (((0,), (0,)), ((), ())), preferred_elemen...  17.4 us
    dot_general x1, matrix products, body(): partial_tan = jnp.dot(acts, low_dir, preferred_element_type=jnp.float32)  16.2 us
  transfers between devices with their start and end apart: 3, of which 3 were waited for; matrix products, arithmetic and copies ran while one was open for 0% of the time, Pallas kernels for 0%

profile of v1, /device:TPU:1, one launch (start us, length us, event | category | flops | bytes accessed | tf_op | source)
XLA Modules:
  0.0 379.2 jit_solution(826784921357248984)
XLA Ops:
  7.2 0.0 all-gather.3.cloned.1.call-start
  7.2 0.7 all-gather.3.cloned.1.call-update
  7.9 0.0 reduce-scatter.2.cloned.1.call-start
  7.9 79.4 %all-gather.3.cloned.1.call-done = bf16[6144,1152]{1,0:T(8,128)(2,1)} async-done(((bf16[768,1152]{1,0:T(8,128)(2,1)}), bf16[6144,1152]{1,0:T(8,128)(2,1)}) %all-gather.3.cloned.1.call-update) | async-done | bytes 14155792 | tf_op jit(solution)/shard_map/all_gather | solution.py:9
  87.3 16.2 %fusion.2 = f32[6144,576]{0,1:T(8,128)} fusion(bf16[6144,1152]{1,0:T(8,128)(2,1)} %all-gather.3.cloned.1.call-done, f32[1152,576]{0,1:T(8,128)} %param.7), kind=kOutput, calls=%fused_computation.10 | convolution fusion | flops 8154390528 | bytes 30965760 | tf_op jit(solution)/shard_map/dot_general | solution.py:10
  103.5 0.0 copy-start
  103.5 0.0 reduce-scatter.2.cloned.1.call-update
  103.5 0.0 all-gather.5.cloned.1.call-start
  103.6 99.8 %reduce-scatter.2.cloned.1.call-done = f32[384,576]{0,1:T(8,128)} async-done(((f32[6144,576]{0,1:T(8,128)}), f32[384,576]{0,1:T(8,128)}) %reduce-scatter.2.cloned.1.call-update) | async-done | bytes 884752 | tf_op jit(solution)/shard_map/reduce_scatter | solution.py:11
  203.4 2.0 convert_element_type.7
  205.3 0.0 all-gather.5.cloned.1.call-update
  205.4 70.8 %all-gather.5.cloned.1.call-done = bf16[6144,576]{0,1:T(8,128)(2,1)} async-done(((bf16[384,576]{0,1:T(8,128)(2,1)}), bf16[6144,576]{0,1:T(8,128)(2,1)}) %all-gather.5.cloned.1.call-update) | async-done | bytes 7077904 | tf_op jit(solution)/shard_map/all_gather | solution.py:12
  276.2 0.0 copy-done
  276.2 17.4 %multiply_reduce_fusion.3 = (f32[]{:T(128)}, f32[]{:T(128)}, f32[]{:T(128)}, f32[]{:T(128)}, f32[1152,576]{0,1:T(8,128)}) fusion(f32[1152,576]{0,1:T(8,128)} %param.6, f32[1152,576]{0,1:T(8,128)S(1)} %copy-done, bf16[6144,576]{0,1:T(8,128)(2,1)} %all-gather.5.cloned.1.call-done, bf16[6144,1152]{1,0:T(8,128)(2,1)} %all-gather.3.cloned.1.call-done), kind=kOutput, calls=%fused_computation.9 | convolution fusion | flops 8160362496 | bytes 29196304 | tf_op jit(solution)/shard_map/dot_general | solution.py:13
  293.5 2.6 pad_maximum_fusion
  296.2 65.1 %psum.7 = f32[4]{0:T(128)S(1)} all-reduce(f32[4]{0:T(128)S(1)} %pad_maximum_fusion), channel_id=1, replica_groups=mesh['dp'=8,'mp'=16] {'dp','mp'}, use_global_device_ids=true, to_apply=%region_5.0 | all-reduce | flops 4 | bytes 32 | tf_op jit(solution)/shard_map/psum | solution.py:25
  361.3 0.7 fusion.4
  365.7 7.0 %multiply_add_fusion = (f32[1152,576]{0,1:T(8,128)}, f32[1152,576]{0,1:T(8,128)}, f32[1152,576]{0,1:T(8,128)}) fusion(f32[1152,576]{0,1:T(8,128)S(1)} %copy-done, f32[]{:T(128)S(6)} %div.18, f32[1152,576]{0,1:T(8,128)} %param.6, f32[1152,576]{0,1:T(8,128)} %get-tuple-element.14, f32[]{:T(128)S(6)} %div.17, f32[1152,576]{0,1:T(8,128)} %param.5), kind=kLoop, calls=%fused_computation.3 | loop fusion | flops 3981312 | bytes 18579464 | tf_op jit(solution)/shard_map/add | solution.py:30
Async XLA Ops:
  7.2 80.2 %all-gather.3.cloned.1.call-start = ((), (), s32[]{:S(2)}) async-start(), calls=%async_computation.1 | async-start | bytes 15925248 | tf_op jit(solution)/shard_map/all_gather | solution.py:9
  7.9 195.5 %reduce-scatter.2.cloned.1.call-start = ((), (), s32[]{:S(2)}) async-start(), calls=%async_computation.2 | async-start | bytes 15040512 | tf_op jit(solution)/shard_map/reduce_scatter | solution.py:11
  103.5 172.7 %copy-start = (f32[1152,576]{0,1:T(8,128)S(1)}, f32[1152,576]{0,1:T(8,128)}, u32[]{:S(2)}) copy-start(f32[1152,576]{0,1:T(8,128)} %param.7) | copy-start | bytes 7962628
  103.5 172.7 %all-gather.5.cloned.1.call-start = ((), (), s32[]{:S(2)}) async-start(), calls=%async_computation.3 | async-start | bytes 7520256 | tf_op jit(solution)/shard_map/all_gather | solution.py:12
Sparse Core Ops, SparseCore 0:
  9.7 77.5 all-gather.2
  103.6 99.6 reduce-scatter.1
  206.3 69.8 all-gather.4

commit v2 on v1

v2 whole, which is shorter than its diff:
```python
import jax
import jax.numpy as jnp
from jax import lax
from jax.experimental import pallas as pl
from jax.experimental.pallas import tpu as pltpu
from jax.sharding import PartitionSpec as P

RING = 4
PIECES = 3
CHUNKS = 2 * RING * PIECES
HOP = 2
LAG = [0, 1, 1 + HOP, 1 + 2 * HOP, 1 + 3 * HOP, 1 + 4 * HOP, 1 + 5 * HOP, 1 + 6 * HOP]
STEPS = CHUNKS + LAG[-1]
MESH = pl.DeviceIdType.MESH


def chunk_place(k):
    late = (k + 18) // 24
    last = (k + 6) // 24
    mid = late - last
    away = mid * (1 + 2 * (k % 2)) + last * 2
    other = (1 - late) * (k // 3) + mid * ((k // 2 + 1) % 2) + last * (k % 2)
    piece = (1 - late) * (k % 3) + mid * ((k + 2) // 4 - 2) + last * (k // 2 - 9)
    return away, other, piece


def kernel(
    acts_ref, res_ref, dir_ref, curved_ref, sums_ref,
    acts, low, tan, part, pass1, got1a, got1b, quad, got2, tiles,
    own_sem, y_send, y_recv, fwd_send, sib_send, sib_recv,
    r1_send, r1_recv, f1_send, f1_recv, r2_send, r2_recv,
    g1_send, g1_recv, g2_send, g2_recv, f2_send, f2_recv,
    sum_send, sum_recv,
):
    dp, mp = lax.axis_index("dp"), lax.axis_index("mp")
    y, c = dp // 2, dp % 2
    z, x = mp // RING, mp % RING
    block = acts_ref.shape[0]
    rows = block // PIECES
    big, small = rows // RING, rows // RING // RING
    tokens = acts.shape[0]
    p1 = x * (1 - c) + z * c
    p2 = z * (1 - c) + x * c
    turn = 1 - 2 * c

    def along_y(d):
        return (((y + d + RING) % RING) * 2 + c, mp)

    def first(d):
        return (dp, ((z + d * c + RING) % RING) * RING + (x + d * (1 - c) + RING) % RING)

    def second(d):
        return (dp, ((z + d * (1 - c)) % RING) * RING + (x + d * c) % RING)

    sibling = (y * 2 + 1 - c, mp)

    def act_rows(away, other, piece):
        who = ((y + away) % RING) * 2 + (c + other) % 2
        return pl.ds(pl.multiple_of(who * block + piece * rows, rows), rows)

    def remote(src, dst, send, recv, to):
        return pltpu.make_async_remote_copy(
            src_ref=src, dst_ref=dst, send_sem=send, recv_sem=recv,
            device_id=to, device_id_type=MESH,
        )

    barrier = pltpu.get_barrier_semaphore()

    @pl.loop(1, 16)
    def _(o):
        pl.semaphore_signal(barrier, inc=1, device_id=(dp, (mp + o) % 16), device_id_type=MESH)

    @pl.loop(1, 8)
    def _(o):
        pl.semaphore_signal(barrier, inc=1, device_id=((dp + o) % 8, mp), device_id_type=MESH)

    for j in range(PIECES):
        pltpu.make_async_copy(
            acts_ref.at[pl.ds(j * rows, rows)], acts.at[act_rows(0, 0, j)], own_sem.at[j]
        ).start()
    low[...] = dir_ref[...].astype(jnp.bfloat16)
    curved_ref[...] = jnp.zeros_like(curved_ref)
    pl.semaphore_wait(barrier, 22)

    def y_copy(j, way):
        here = acts.at[act_rows(0, 0, j)]
        arrives = 1 + 2 * way
        return remote(
            here, here, y_send.at[way, j], y_recv.at[arrives, j], along_y(2 * way - 1)
        )

    def sib_copy(away, j):
        here = acts.at[act_rows(away, 0, j)]
        return remote(here, here, sib_send.at[away, j], sib_recv.at[away, j], sibling)

    def fwd_copy(j):
        here = acts.at[act_rows((RING - turn) % RING, 0, j)]
        return remote(here, here, fwd_send.at[j], y_recv.at[2, j], along_y(turn))

    for j in range(PIECES):
        pltpu.make_async_copy(
            acts_ref.at[pl.ds(j * rows, rows)], acts.at[act_rows(0, 0, j)], own_sem.at[j]
        ).wait()
        y_copy(j, 0).start()
        y_copy(j, 1).start()
        sib_copy(0, j).start()

    def part_rows(k, slot):
        return pl.ds(pl.multiple_of(k * rows + slot * big, 16), big)

    def quad_rows(k, slot):
        return pl.ds(pl.multiple_of(k * big + slot * small, 16), small)

    def tan_rows(k, slot, sub):
        return pl.ds(pl.multiple_of(k * rows + slot * big + sub * small, 16), small)

    def big_rows(k):
        return pl.ds(pl.multiple_of(k * big, 16), big)

    def two_rows(k, o):
        return pl.ds(pl.multiple_of((k * 3 + o - 1) * small, 16), small)

    def way_of(k):
        return 1 - 2 * (k % 2)

    def r1_copy(k, which):
        s = way_of(k)
        if which == 0:
            src = part.at[part_rows(k, (p1 + 2) % RING)]
            return remote(src, pass1.at[big_rows(k)], r1_send.at[k, 0], r1_recv.at[k, 0], first(s))
        src = part.at[part_rows(k, (p1 + RING - s) % RING)]
        return remote(src, got1b.at[big_rows(k)], r1_send.at[k, 1], r1_recv.at[k, 1], first(-s))

    def f1_copy(k):
        s = way_of(k)
        src = part.at[part_rows(k, (p1 + RING + s) % RING)]
        return remote(src, got1a.at[big_rows(k)], f1_send.at[k], f1_recv.at[k], first(s))

    def r2_copy(k, o):
        src = quad.at[quad_rows(k, (p2 + o) % RING)]
        return remote(
            src, got2.at[two_rows(k, o)], r2_send.at[k, o - 1], r2_recv.at[k, o - 1], second(o)
        )

    def g1_copy(k, o, whose):
        here = tan.at[tan_rows(k, p1, whose)]
        return remote(here, here, g1_send.at[k, o - 1], g1_recv.at[k, o - 1], second(o))

    def g2_copy(k, way, whose):
        here = tan.at[part_rows(k, whose)]
        to = first(way_of(k) * (1 - 2 * way))
        return remote(here, here, g2_send.at[k, way], g2_recv.at[k, way], to)

    def f2_copy(k, whose):
        here = tan.at[part_rows(k, whose)]
        return remote(here, here, f2_send.at[k], f2_recv.at[k], first(way_of(k)))

    def arrive(k):
        away, other, piece = chunk_place(k)

        @pl.when((other == 0) & (away != 0))
        def _():
            here = acts.at[act_rows(away, 0, piece)]
            remote(
                here, here, y_send.at[0, 0], y_recv.at[away, piece], sibling
            ).wait_recv()
            sib_copy(away, piece).start()

            @pl.when(away == (RING - turn) % RING)
            def _():
                fwd_copy(piece).start()

        @pl.when(other == 1)
        def _():
            here = acts.at[act_rows(away, 1, piece)]
            remote(
                here, here, sib_send.at[0, 0], sib_recv.at[away, piece], sibling
            ).wait_recv()

    def forward_product(k):
        away, other, piece = chunk_place(k)
        product = jnp.dot(
            acts[act_rows(away, other, piece), :], low[...], preferred_element_type=jnp.float32
        )
        part[pl.ds(pl.multiple_of(k * rows, rows), rows), :] = product.astype(jnp.bfloat16)
        r1_copy(k, 0).start()
        r1_copy(k, 1).start()

    def pass_on(k):
        r1_copy(k, 0).wait_recv()
        here = part_rows(k, (p1 + RING + way_of(k)) % RING)
        part[here, :] = (
            part[here, :].astype(jnp.float32) + pass1[big_rows(k), :].astype(jnp.float32)
        ).astype(jnp.bfloat16)
        f1_copy(k).start()

    def quarter(k):
        f1_copy(k).wait_recv()
        r1_copy(k, 1).wait_recv()
        quad[big_rows(k), :] = (
            part[part_rows(k, p1), :].astype(jnp.float32)
            + got1a[big_rows(k), :].astype(jnp.float32)
            + got1b[big_rows(k), :].astype(jnp.float32)
        ).astype(jnp.bfloat16)
        for o in range(1, RING):
            r2_copy(k, o).start()

    def total(k):
        value = quad[quad_rows(k, p2), :].astype(jnp.float32)
        for o in range(1, RING):
            r2_copy(k, o).wait_recv()
            value = value + got2[two_rows(k, o), :].astype(jnp.float32)
        tan[tan_rows(k, p1, p2), :] = value.astype(jnp.bfloat16)
        for o in range(1, RING):
            g1_copy(k, o, p2).start()

    def spread(k):
        for o in range(1, RING):
            g1_copy(k, o, (p2 + RING - o) % RING).wait_recv()
        g2_copy(k, 0, p1).start()
        g2_copy(k, 1, p1).start()

    def spread_on(k):
        whose = (p1 + RING - way_of(k)) % RING
        g2_copy(k, 0, whose).wait_recv()
        f2_copy(k, whose).start()

    def back_product(k):
        s = way_of(k)
        g2_copy(k, 1, (p1 + RING + s) % RING).wait_recv()
        f2_copy(k, (p1 + 2) % RING).wait_recv()
        away, other, piece = chunk_place(k)
        t = tan[pl.ds(pl.multiple_of(k * rows, rows), rows), :]
        width = 384

        @pl.loop(0, acts.shape[1] // width)
        def _(h):
            cols = pl.ds(pl.multiple_of(h * width, width), width)
            curved_ref[cols, :] += lax.dot_general(
                acts[act_rows(away, other, piece), cols], t, (((0,), (0,)), ((), ())),
                preferred_element_type=jnp.float32,
            )

        r1_copy(k, 0).wait_send()
        r1_copy(k, 1).wait_send()
        f1_copy(k).wait_send()
        for o in range(1, RING):
            r2_copy(k, o).wait_send()
            g1_copy(k, o, p2).wait_send()
        g2_copy(k, 0, p1).wait_send()
        g2_copy(k, 1, p1).wait_send()
        f2_copy(k, (p1 + RING - s) % RING).wait_send()

    stages = [
        (2, pass_on), (3, quarter), (4, total), (5, spread), (6, spread_on),
        (0, arrive), (1, forward_product), (7, back_product),
    ]

    @pl.loop(0, STEPS)
    def _(step):
        for at, stage in stages:
            k = step - LAG[at]

            @pl.when((k >= 0) & (k < CHUNKS))
            def _(k=k, stage=stage):
                stage(k)

    for j in range(PIECES):
        y_copy(j, 0).wait_send()
        y_copy(j, 1).wait_send()
        fwd_copy(j).wait_send()
        for away in range(RING):
            sib_copy(away, j).wait_send()

    direction, residual = dir_ref[...], res_ref[...]
    curved = curved_ref[...] / tokens + 1.0 * direction
    curved_ref[...] = curved

    def line(v):
        one = jnp.sum(jnp.sum(v, axis=0, keepdims=True), axis=1, keepdims=True)
        return jnp.broadcast_to(one, (1, 128))

    mine = jnp.concatenate(
        [line(residual * residual), line(direction * curved), line(residual * curved),
         line(curved * curved), jnp.zeros((4, 128), jnp.float32)], axis=0,
    )
    tiles[mp] = mine

    def plane_copy(o, whose):
        here = tiles.at[whose]
        return remote(here, here, sum_send.at[o], sum_recv.at[o], (dp, (mp + o) % 16))

    def column_copy(o, whose):
        here = tiles.at[16 + whose]
        return remote(here, here, sum_send.at[16 + o], sum_recv.at[16 + o], ((dp + o) % 8, mp))

    @pl.loop(1, 16)
    def _(o):
        plane_copy(o, mp).start()

    @pl.loop(1, 16)
    def _(o):
        plane_copy(o, (mp + 16 - o) % 16).wait_recv()

    subtotal = tiles[0]
    for i in range(1, 16):
        subtotal = subtotal + tiles[i]
    tiles[16 + dp] = subtotal

    @pl.loop(1, 8)
    def _(o):
        column_copy(o, dp).start()

    @pl.loop(1, 8)
    def _(o):
        column_copy(o, (dp + 8 - o) % 8).wait_recv()

    whole = tiles[16]
    for i in range(1, 8):
        whole = whole + tiles[16 + i]
    sums_ref[...] = whole

    @pl.loop(1, 16)
    def _(o):
        plane_copy(o, mp).wait_send()

    @pl.loop(1, 8)
    def _(o):
        column_copy(o, dp).wait_send()


def curvature(saved_acts, residual, direction):
    block, hidden = saved_acts.shape
    columns = direction.shape[1]
    rows = block // PIECES
    big, small = rows // RING, rows // RING // RING
    bf16, f32 = jnp.bfloat16, jnp.float32
    dma = pltpu.SemaphoreType.DMA
    vmem = pl.BlockSpec(memory_space=pltpu.VMEM)
    return pl.pallas_call(
        kernel,
        out_shape=(
            jax.ShapeDtypeStruct((hidden, columns), f32),
            jax.ShapeDtypeStruct((8, 128), f32),
        ),
        in_specs=[pl.BlockSpec(memory_space=pl.ANY), vmem, vmem],
        out_specs=(vmem, vmem),
        scratch_shapes=[
            pltpu.VMEM((8 * block, hidden), bf16),
            pltpu.VMEM((hidden, columns), bf16),
            pltpu.VMEM((CHUNKS * rows, columns), bf16),
            pltpu.VMEM((CHUNKS * rows, columns), bf16),
            pltpu.VMEM((CHUNKS * big, columns), bf16),
            pltpu.VMEM((CHUNKS * big, columns), bf16),
            pltpu.VMEM((CHUNKS * big, columns), bf16),
            pltpu.VMEM((CHUNKS * big, columns), bf16),
            pltpu.VMEM((CHUNKS * 3 * small, columns), bf16),
            pltpu.VMEM((24, 8, 128), f32),
            dma((PIECES,)), dma((2, PIECES)), dma((RING, PIECES)), dma((PIECES,)),
            dma((RING, PIECES)), dma((RING, PIECES)),
            dma((CHUNKS, 2)), dma((CHUNKS, 2)), dma((CHUNKS,)), dma((CHUNKS,)),
            dma((CHUNKS, 3)), dma((CHUNKS, 3)), dma((CHUNKS, 3)), dma((CHUNKS, 3)),
            dma((CHUNKS, 2)), dma((CHUNKS, 2)), dma((CHUNKS,)), dma((CHUNKS,)),
            dma((24,)), dma((24,)),
        ],
        compiler_params=pltpu.CompilerParams(
            collective_id=0, has_side_effects=True, vmem_limit_bytes=62 * 2**20
        ),
        cost_estimate=pl.CostEstimate(
            flops=32 * block * hidden * columns, bytes_accessed=16 * 2**20, transcendentals=0
        ),
    )(saved_acts, residual, direction)


def body(saved_acts, solution, residual, direction):
    curved, sums = curvature(saved_acts, residual, direction)
    norm_old, along, res_curved, curved_sq = sums[0, 0], sums[1, 0], sums[2, 0], sums[3, 0]
    step_size = norm_old / along
    new_residual = residual - step_size * curved
    norm_new = norm_old + step_size * (step_size * curved_sq - 2.0 * res_curved)
    new_solution = solution + step_size * direction
    new_direction = new_residual + norm_new / norm_old * direction
    return (new_solution, new_residual, new_direction)


def solution(mesh):
    return jax.shard_map(
        body,
        mesh=mesh,
        in_specs=(P("dp", "mp"), P("mp", "dp"), P("mp", "dp"), P("mp", "dp")),
        out_specs=(P("mp", "dp"), P("mp", "dp"), P("mp", "dp")),
        check_vma=False,
    )
```

time: 380 us -> 170 us (0.45)
  waiting for transfers between devices: 251 us -> 0 us
  Pallas kernels: 0 us -> 138 us
  blocking collectives: 65.1 us -> 0 us
  matrix products: 33.5 us -> 0 us
  local copies, waits for them, and re-layouts: 0.67 us -> 20.3 us
  between operations: 17.5 us -> 4.59 us
  other arithmetic: 11.6 us -> 7.67 us
    all_gather x2 -> x0, waiting for transfers between devices: 150 us -> none  [the longest x1 79.4 us: body(): acts = lax.all_gather(saved_acts, 'dp', axis=0, tiled=True)]
    pallas_call x0 -> x1, Pallas kernels: none -> 138 us  [curvature(): pl.pallas_call(kernel, out_shape=(jax.ShapeDtypeStruct((hidden, columns),...]
    reduce_scatter x1 -> x0, waiting for transfers between devices: 99.8 us -> none  [body(): mine = lax.psum_scatter(partial_tan, 'mp', scatter_dimension=0, tiled=True)]
    psum x1 -> x0, blocking collectives: 65.1 us -> none  [body(): norm_old, along, res_curved, curved_sq = lax.psum(sums, ('dp', 'mp'))]
    dot_general x2 -> x0, matrix products: 33.5 us -> none  [the longest x1 17.4 us: body(): lax.dot_general(acts, tangent, (((0,), (0,)), ((), ())), preferred_elemen...]
    unnamed x2 -> x12, local copies, waits for them, and re-layouts: 0.01 us -> 18.9 us
  transfers between devices with their start and end apart: 3 -> 0, of which waited for: 3 -> 0; matrix products, arithmetic and copies ran while one was open for 0% -> 0% of each run, Pallas kernels for 0% -> 0%
where the time goes in v2:
time: 170 us
  Pallas kernels  138 us (81%)
  local copies, waits for them, and re-layouts  20.3 us (12%)
  other arithmetic  7.67 us (5%)
  between operations  4.59 us (3%)
    pallas_call x1, Pallas kernels, curvature(): pl.pallas_call(kernel, out_shape=(jax.ShapeDtypeStruct((hidden, columns),...  138 us
    unnamed x12, local copies, waits for them, and re-layouts  18.9 us
    add x1, other arithmetic, body(): new_direction = new_residual + norm_new / norm_old * direction  7.67 us

profile of v2, /device:TPU:1, one launch (start us, length us, event | category | flops | bytes accessed | tf_op | source)
XLA Modules:
  0.0 170.2 jit_solution(14565144981004157336)
XLA Ops:
  0.6 0.0 copy-start.2
  0.6 3.7 %copy.7.res_ref = f32[1152,576]{1,0:T(8,128)} copy(f32[1152,576]{0,1:T(8,128)} %param.6) | data formatting | bytes 5308416 | tf_op args[2]
  4.4 0.0 copy-done.2
  4.4 2.4 %copy.8.dir_ref = f32[1152,576]{1,0:T(8,128)} copy(f32[1152,576]{0,1:T(8,128)S(1)} %copy-done.2) | data formatting | bytes 5308416 | tf_op args[3]
  6.7 137.7 %shard_map.67 = (f32[1152,576]{1,0:T(8,128)}, f32[8,128]{1,0:T(8,128)}) custom-call(bf16[768,1152]{1,0:T(8,128)(2,1)} %acts_ref.1, f32[1152,576]{1,0:T(8,128)} %copy.7.res_ref, f32[1152,576]{1,0:T(8,128)} %copy.8.dir_ref), custom_call_target="tpu_custom_call" | custom-call | flops 16307453952 | bytes 16777216 | tf_op jit(solution)/shard_map/pallas_call | solution.py:340
  144.4 0.0 copy-start
  144.4 1.4 fusion
  149.7 3.5 %copy.10 = f32[1152,576]{1,0:T(8,128)} copy(f32[1152,576]{0,1:T(8,128)} %param.5) | data formatting | bytes 5308416 | tf_op args[1]
  153.2 0.0 copy-done
  153.2 7.7 %multiply_add_fusion = (f32[1152,576]{1,0:T(8,128)}, f32[1152,576]{1,0:T(8,128)}, f32[1152,576]{1,0:T(8,128)}) fusion(f32[1152,576]{1,0:T(8,128)} %copy.8.dir_ref, f32[]{:T(128)S(6)} %div.7, f32[1152,576]{1,0:T(8,128)S(1)} %copy-done, f32[1152,576]{1,0:T(8,128)} %get-tuple-element.6, f32[]{:T(128)S(6)} %div.6, f32[1152,576]{1,0:T(8,128)} %copy.10), kind=kLoop, calls=%fused_computation | loop fusion | flops 3981312 | bytes 18579464 | tf_op jit(solution)/shard_map/add | solution.py:382
  160.9 3.4 %copy.13 = f32[1152,576]{0,1:T(8,128)} copy(f32[1152,576]{1,0:T(8,128)} %get-tuple-element.12) | data formatting | bytes 5308416
  164.3 0.0 copy-start.1
  164.3 3.6 %copy.14 = f32[1152,576]{0,1:T(8,128)} copy(f32[1152,576]{1,0:T(8,128)} %get-tuple-element.11) | data formatting | bytes 5308416
  167.9 0.0 copy-done.1
  167.9 2.3 %copy.15 = f32[1152,576]{0,1:T(8,128)} copy(f32[1152,576]{1,0:T(8,128)S(1)} %copy-done.1) | data formatting | bytes 5308416
Async XLA Ops:
  0.6 3.7 %copy-start.2 = (f32[1152,576]{0,1:T(8,128)S(1)}, f32[1152,576]{0,1:T(8,128)}, u32[]{:S(2)}) copy-start(f32[1152,576]{0,1:T(8,128)} %param.7) | copy-start | bytes 7962628
  144.4 8.8 %copy-start = (f32[1152,576]{1,0:T(8,128)S(1)}, f32[1152,576]{1,0:T(8,128)}, u32[]{:S(2)}) copy-start(f32[1152,576]{1,0:T(8,128)} %copy.7.res_ref) | copy-start | bytes 7962628
  164.3 3.6 %copy-start.1 = (f32[1152,576]{1,0:T(8,128)S(1)}, f32[1152,576]{1,0:T(8,128)}, u32[]{:S(2)}) copy-start(f32[1152,576]{1,0:T(8,128)} %get-tuple-element.10) | copy-start | bytes 7962628

commit v3 on v2

v3 whole, which is shorter than its diff:
```python
import jax
import jax.numpy as jnp
from jax import lax
from jax.experimental import pallas as pl
from jax.experimental.pallas import tpu as pltpu
from jax.sharding import PartitionSpec as P

RING = 4
PIECES = 3
CHUNKS = 2 * RING * PIECES
PAIRS = CHUNKS // 2
HOP = 3
SEND_AT = (6, 12)
LAG = [0, 1, 1 + HOP, 1 + 2 * HOP, 1 + 3 * HOP, 1 + 4 * HOP, 1 + 5 * HOP, 1 + 6 * HOP]
REST = 6
STEPS = CHUNKS + REST + LAG[-1]
MESH = pl.DeviceIdType.MESH


def chunk_place(k):
    late = (k + 18) // 24
    last = (k + 6) // 24
    mid = late - last
    away = mid * (1 + 2 * (k % 2)) + last * 2
    other = (1 - late) * (k // 3) + mid * ((k // 2 + 1) % 2) + last * (k % 2)
    piece = (1 - late) * (k % 3) + mid * ((k + 2) // 4 - 2) + last * (k // 2 - 9)
    return away, other, piece


def kernel(
    acts_ref, res_ref, dir_ref, curved_ref, sums_ref,
    acts, low, tan, part, pass1, got1a, got1b, quad, got2, tiles, dir_here, res_here,
    own_sem, y_send, y_recv, fwd_send, sib_send, sib_recv,
    sent, r1_recv, f1_recv, r2_recv, g1_recv, g2_recv, f2_recv,
    sum_send, sum_recv,
):
    dp, mp = lax.axis_index("dp"), lax.axis_index("mp")
    y, c = dp // 2, dp % 2
    z, x = mp // RING, mp % RING
    block = acts_ref.shape[0]
    rows = block // PIECES
    cols = low.shape[0]
    big = cols // RING
    lanes = 2 * rows // RING
    tokens = acts.shape[0]
    p1 = x * (1 - c) + z * c
    p2 = z * (1 - c) + x * c
    turn = 1 - 2 * c

    def along_y(d):
        return (((y + d + RING) % RING) * 2 + c, mp)

    def first(d):
        return (dp, ((z + d * c + RING) % RING) * RING + (x + d * (1 - c) + RING) % RING)

    def second(d):
        return (dp, ((z + d * (1 - c)) % RING) * RING + (x + d * c) % RING)

    sibling = (y * 2 + 1 - c, mp)

    def act_rows(away, other, piece):
        who = ((y + away) % RING) * 2 + (c + other) % 2
        return pl.ds(pl.multiple_of(who * block + piece * rows, rows), rows)

    def remote(src, dst, send, recv, to):
        return pltpu.make_async_remote_copy(
            src_ref=src, dst_ref=dst, send_sem=send, recv_sem=recv,
            device_id=to, device_id_type=MESH,
        )

    def own_copy(j):
        return pltpu.make_async_copy(
            acts_ref.at[pl.ds(j * rows, rows)], acts.at[act_rows(0, 0, j)], own_sem.at[j]
        )

    load_dir = pltpu.make_async_copy(dir_ref, dir_here, own_sem.at[PIECES])
    load_res = pltpu.make_async_copy(res_ref, res_here, own_sem.at[PIECES + 1])
    load_dir.start()
    for j in range(PIECES):
        own_copy(j).start()
    load_res.start()
    barrier = pltpu.get_barrier_semaphore()

    @pl.loop(1, 16)
    def _(o):
        pl.semaphore_signal(barrier, inc=1, device_id=(dp, (mp + o) % 16), device_id_type=MESH)

    @pl.loop(1, 8)
    def _(o):
        pl.semaphore_signal(barrier, inc=1, device_id=((dp + o) % 8, mp), device_id_type=MESH)

    load_dir.wait()
    low[...] = dir_here[...].astype(jnp.bfloat16)
    curved_ref[...] = jnp.zeros_like(curved_ref)
    pl.semaphore_wait(barrier, 22)

    def y_copy(j, way):
        here = acts.at[act_rows(0, 0, j)]
        arrives = 1 + 2 * way
        return remote(
            here, here, y_send.at[way, j], y_recv.at[arrives, j], along_y(2 * way - 1)
        )

    def sib_copy(away, j):
        here = acts.at[act_rows(away, 0, j)]
        return remote(here, here, sib_send.at[away, j], sib_recv.at[away, j], sibling)

    def fwd_copy(j):
        here = acts.at[act_rows((RING - turn) % RING, 0, j)]
        return remote(here, here, fwd_send.at[j], y_recv.at[2, j], along_y(turn))

    for j in range(PIECES):
        own_copy(j).wait()
        sib_copy(0, j).start()
        if j == 0:
            y_copy(j, 0).start()
            y_copy(j, 1).start()

    def slot_rows(slot):
        return pl.ds(pl.multiple_of(slot * big, 16), big)

    def lane(slot):
        return pl.ds(pl.multiple_of(slot * lanes, lanes), lanes)

    def way_of(k):
        return 1 - 2 * (k % 2)

    def r1_copy(k, which):
        s = way_of(k)
        if which == 0:
            src = part.at[k, slot_rows((p1 + 2) % RING)]
            return remote(src, pass1.at[k], sent.at[k // 2], r1_recv.at[k, 0], first(s))
        src = part.at[k, slot_rows((p1 + RING - s) % RING)]
        return remote(src, got1b.at[k], sent.at[k // 2], r1_recv.at[k, 1], first(-s))

    def f1_copy(k):
        s = way_of(k)
        src = part.at[k, slot_rows((p1 + RING + s) % RING)]
        return remote(src, got1a.at[k], sent.at[k // 2], f1_recv.at[k], first(s))

    def r2_copy(m, o):
        src = quad.at[m, :, lane((p2 + o) % RING)]
        return remote(src, got2.at[m, o - 1], sent.at[m], r2_recv.at[m], second(o))

    def g1_copy(m, o):
        here = tan.at[m, slot_rows(p1), lane(p2)]
        return remote(here, here, sent.at[m], g1_recv.at[m], second(o))

    def g2_copy(m, way, whose):
        here = tan.at[m, slot_rows(whose)]
        to = first(way_of(m) * (1 - 2 * way))
        return remote(here, here, sent.at[m], g2_recv.at[m, way], to)

    def f2_copy(m, whose):
        here = tan.at[m, slot_rows(whose)]
        return remote(here, here, sent.at[m], f2_recv.at[m], first(way_of(m)))

    def wait_all(sem, some):
        pltpu.make_async_copy(some, some, sem).wait()

    def arrive(k):
        away, other, piece = chunk_place(k)

        @pl.when((other == 0) & (away != 0))
        def _():
            here = acts.at[act_rows(away, 0, piece)]
            remote(
                here, here, y_send.at[0, 0], y_recv.at[away, piece], sibling
            ).wait_recv()
            sib_copy(away, piece).start()

            @pl.when(away == (RING - turn) % RING)
            def _():
                fwd_copy(piece).start()

        @pl.when(other == 1)
        def _():
            here = acts.at[act_rows(away, 1, piece)]
            remote(
                here, here, sib_send.at[0, 0], sib_recv.at[away, piece], sibling
            ).wait_recv()

    def forward_product(k):
        product = lax.dot_general(
            low[...], acts[act_rows(*chunk_place(k)), :], (((1,), (1,)), ((), ())),
            preferred_element_type=jnp.float32,
        )
        part[k] = product.astype(jnp.bfloat16)
        r1_copy(k, 0).start()
        r1_copy(k, 1).start()

    def pass_on(k):
        r1_copy(k, 0).wait_recv()
        here = slot_rows((p1 + RING + way_of(k)) % RING)
        part[k, here, :] = (
            part[k, here, :].astype(jnp.float32) + pass1[k].astype(jnp.float32)
        ).astype(jnp.bfloat16)
        f1_copy(k).start()

    def quarter(k):
        f1_copy(k).wait_recv()
        r1_copy(k, 1).wait_recv()
        half = pl.ds(pl.multiple_of((k % 2) * rows, rows), rows)
        quad[k // 2, :, half] = (
            part[k, slot_rows(p1), :].astype(jnp.float32)
            + got1a[k].astype(jnp.float32)
            + got1b[k].astype(jnp.float32)
        ).astype(jnp.bfloat16)

        @pl.when(k % 2 == 1)
        def _():
            for o in range(1, RING):
                r2_copy(k // 2, o).start()

    def total(m):
        wait_all(r2_recv.at[m], got2.at[m])
        value = quad[m, :, lane(p2)].astype(jnp.float32)
        for o in range(1, RING):
            value = value + got2[m, o - 1].astype(jnp.float32)
        tan[m, slot_rows(p1), lane(p2)] = value.astype(jnp.bfloat16)
        for o in range(1, RING):
            g1_copy(m, o).start()

    def spread(m):
        wait_all(g1_recv.at[m], got2.at[m])
        g2_copy(m, 0, p1).start()
        g2_copy(m, 1, p1).start()

    def spread_on(m):
        whose = (p1 + RING - way_of(m)) % RING
        g2_copy(m, 0, whose).wait_recv()
        f2_copy(m, whose).start()

    def back_product(m):
        g2_copy(m, 1, (p1 + RING + way_of(m)) % RING).wait_recv()
        f2_copy(m, (p1 + 2) % RING).wait_recv()

        @pl.loop(0, acts.shape[1] // WIDE)
        def _(h):
            at = pl.ds(pl.multiple_of(h * WIDE, WIDE), WIDE)
            curved_ref[:, at] += jnp.dot(
                tan[m, :, 0:rows], acts[act_rows(*chunk_place(2 * m)), at],
                preferred_element_type=jnp.float32,
            ) + jnp.dot(
                tan[m, :, rows : 2 * rows], acts[act_rows(*chunk_place(2 * m + 1)), at],
                preferred_element_type=jnp.float32,
            )

        wait_all(sent.at[m], part.at[2 * m])
        wait_all(sent.at[m], part.at[2 * m, pl.ds(0, 2 * big)])
        wait_all(sent.at[m], got2.at[m])
        wait_all(sent.at[m], got2.at[m])
        wait_all(sent.at[m], tan.at[m, pl.ds(0, 3 * big)])

    stages = [
        (2, pass_on, 1), (3, quarter, 1), (4, total, 2), (5, spread, 2), (6, spread_on, 2),
        (0, arrive, 1), (1, forward_product, 1), (7, back_product, 2),
    ]

    @pl.loop(0, STEPS)
    def _(step):
        for j, at in ((1, SEND_AT[0]), (2, SEND_AT[1])):

            @pl.when(step == at)
            def _(j=j):
                y_copy(j, 0).start()
                y_copy(j, 1).start()

        for at, stage, every in stages:
            turn_of = step - LAG[at]
            rested = (turn_of + 64 - 2 * PIECES - REST) // 64
            k = turn_of - rested * REST

            @pl.when(
                (k >= 0) & (k < CHUNKS) & ((rested == 1) | (k < 2 * PIECES))
                & (k % every == every - 1)
            )
            def _(k=k, stage=stage, every=every):
                stage(k // every)

    for j in range(PIECES):
        y_copy(j, 0).wait_send()
        y_copy(j, 1).wait_send()
        fwd_copy(j).wait_send()
        for away in range(RING):
            sib_copy(away, j).wait_send()

    load_res.wait()
    direction, residual = dir_here[...], res_here[...]
    curved = curved_ref[...] / tokens + 1.0 * direction
    curved_ref[...] = curved

    def total_of(v):
        return jnp.sum(jnp.sum(v, axis=0, keepdims=True), axis=1, keepdims=True)

    place = lax.broadcasted_iota(jnp.int32, (1, 128), 1)
    mine = jnp.zeros((1, 128), jnp.float32)
    for i, (a, b) in enumerate(
        ((residual, residual), (direction, curved), (residual, curved), (curved, curved))
    ):
        mine = jnp.where(place == i, total_of(a * b), mine)
    tiles[mp] = mine

    def plane_copy(o, whose):
        here = tiles.at[whose]
        return remote(here, here, sum_send.at[o], sum_recv.at[o], (dp, (mp + o) % 16))

    def column_copy(o, whose):
        here = tiles.at[16 + whose]
        return remote(here, here, sum_send.at[16 + o], sum_recv.at[16 + o], ((dp + o) % 8, mp))

    @pl.loop(1, 16)
    def _(o):
        plane_copy(o, mp).start()

    @pl.loop(1, 16)
    def _(o):
        plane_copy(o, (mp + 16 - o) % 16).wait_recv()

    subtotal = tiles[0]
    for i in range(1, 16):
        subtotal = subtotal + tiles[i]
    tiles[16 + dp] = subtotal

    @pl.loop(1, 8)
    def _(o):
        column_copy(o, dp).start()

    @pl.loop(1, 8)
    def _(o):
        column_copy(o, (dp + 8 - o) % 8).wait_recv()

    whole = tiles[16]
    for i in range(1, 8):
        whole = whole + tiles[16 + i]
    sums_ref[...] = jnp.broadcast_to(whole, (8, 128))

    @pl.loop(1, 16)
    def _(o):
        plane_copy(o, mp).wait_send()

    @pl.loop(1, 8)
    def _(o):
        column_copy(o, dp).wait_send()


WIDE = 384


def curvature(saved_acts, residual, direction):
    block, hidden = saved_acts.shape
    columns = direction.shape[0]
    rows = block // PIECES
    big, lanes = columns // RING, 2 * rows // RING
    bf16, f32 = jnp.bfloat16, jnp.float32
    dma = pltpu.SemaphoreType.DMA
    vmem = pl.BlockSpec(memory_space=pltpu.VMEM)
    return pl.pallas_call(
        kernel,
        out_shape=(
            jax.ShapeDtypeStruct((columns, hidden), f32),
            jax.ShapeDtypeStruct((8, 128), f32),
        ),
        in_specs=[pl.BlockSpec(memory_space=pltpu.HBM)] * 3,
        out_specs=(vmem, vmem),
        scratch_shapes=[
            pltpu.VMEM((8 * block, hidden), bf16),
            pltpu.VMEM((columns, hidden), bf16),
            pltpu.VMEM((PAIRS, columns, 2 * rows), bf16),
            pltpu.VMEM((CHUNKS, columns, rows), bf16),
            pltpu.VMEM((CHUNKS, big, rows), bf16),
            pltpu.VMEM((CHUNKS, big, rows), bf16),
            pltpu.VMEM((CHUNKS, big, rows), bf16),
            pltpu.VMEM((PAIRS, big, 2 * rows), bf16),
            pltpu.VMEM((PAIRS, 3, big, lanes), bf16),
            pltpu.VMEM((24, 1, 128), f32),
            pltpu.VMEM((columns, hidden), f32),
            pltpu.VMEM((columns, hidden), f32),
            dma((PIECES + 2,)), dma((2, PIECES)), dma((RING, PIECES)), dma((PIECES,)),
            dma((RING, PIECES)), dma((RING, PIECES)),
            dma((PAIRS,)), dma((CHUNKS, 2)), dma((CHUNKS,)), dma((PAIRS,)), dma((PAIRS,)),
            dma((PAIRS, 2)), dma((PAIRS,)),
            dma((24,)), dma((24,)),
        ],
        compiler_params=pltpu.CompilerParams(
            collective_id=0, has_side_effects=True, vmem_limit_bytes=46 * 2**20
        ),
        cost_estimate=pl.CostEstimate(
            flops=32 * block * hidden * columns, bytes_accessed=16 * 2**20, transcendentals=0
        ),
    )(saved_acts, residual, direction)


def finish_kernel(sums_ref, curved_ref, sol_ref, res_ref, dir_ref, *refs):
    outs, here, sems = refs[:3], refs[3:6], refs[6]
    norm_old, along = sums_ref[0:1, 0:1], sums_ref[0:1, 1:2]
    res_curved, curved_sq = sums_ref[0:1, 2:3], sums_ref[0:1, 3:4]
    step_size = norm_old / along
    norm_new = norm_old + step_size * (step_size * curved_sq - 2.0 * res_curved)
    growth = norm_new / norm_old
    blocks = 4
    size = curved_ref.shape[0] // blocks
    copies = []
    for i in range(blocks):
        at = pl.ds(i * size, size)
        direction = dir_ref[at, :]
        new_residual = res_ref[at, :] - step_size * curved_ref[at, :]
        here[0][at, :] = sol_ref[at, :] + step_size * direction
        here[1][at, :] = new_residual
        here[2][at, :] = new_residual + growth * direction
        for o in range(3):
            copy = pltpu.make_async_copy(here[o].at[at], outs[o].at[at], sems.at[o, i])
            copy.start()
            copies.append(copy)
    for copy in copies:
        copy.wait()


def finish(sums, curved, solution, residual, direction):
    vmem = pl.BlockSpec(memory_space=pltpu.VMEM)
    field = jax.ShapeDtypeStruct(curved.shape, jnp.float32)
    return pl.pallas_call(
        finish_kernel,
        out_shape=(field,) * 3,
        in_specs=[vmem] * 5,
        out_specs=(pl.BlockSpec(memory_space=pltpu.HBM),) * 3,
        scratch_shapes=[pltpu.VMEM(curved.shape, jnp.float32)] * 3
        + [pltpu.SemaphoreType.DMA((3, 4))],
        compiler_params=pltpu.CompilerParams(vmem_limit_bytes=40 * 2**20),
    )(sums, curved, solution, residual, direction)


def body(saved_acts, solution, residual, direction):
    solution, residual, direction = solution.T, residual.T, direction.T
    curved, sums = curvature(saved_acts, residual, direction)
    outs = finish(sums, curved, solution, residual, direction)
    return tuple(out.T for out in outs)


def solution(mesh):
    return jax.shard_map(
        body,
        mesh=mesh,
        in_specs=(P("dp", "mp"), P("mp", "dp"), P("mp", "dp"), P("mp", "dp")),
        out_specs=(P("mp", "dp"), P("mp", "dp"), P("mp", "dp")),
        check_vma=False,
    )
```

time: 170 us -> 130 us (0.76)
  local copies, waits for them, and re-layouts: 20.3 us -> 3.23 us
  Pallas kernels: 138 us -> 126 us
  other arithmetic: 7.67 us -> 0 us
  between operations: 4.59 us -> 0.67 us
    unnamed x12 -> x10, local copies, waits for them, and re-layouts: 18.9 us -> 3.23 us
    pallas_call x1 -> x2, Pallas kernels: 138 us -> 126 us  [the longest x1 122 us: curvature(): pl.pallas_call(kernel, out_shape=(jax.ShapeDtypeStruct((columns, hidden),...]
    add x1 -> x0, other arithmetic: 7.67 us -> none  [body(): new_direction = new_residual + norm_new / norm_old * direction]
where the time goes in v3:
time: 130 us
  Pallas kernels  126 us (97%)
  local copies, waits for them, and re-layouts  3.23 us (2%)
    pallas_call x1, Pallas kernels, curvature(): pl.pallas_call(kernel, out_shape=(jax.ShapeDtypeStruct((columns, hidden),...  122 us
    pallas_call x1, Pallas kernels, finish(): pl.pallas_call(finish_kernel, out_shape=(field,) * 3, in_specs=[vmem] * 5...  3.49 us
    unnamed x10, local copies, waits for them, and re-layouts  3.23 us

profile of v3, /device:TPU:1, one launch (start us, length us, event | category | flops | bytes accessed | tf_op | source)
XLA Modules:
  0.0 129.7 jit_solution(2026466538840874168)
XLA Ops:
  0.6 0.0 copy-start
  0.6 1.7 %copy-done = f32[1152,576]{0,1:T(8,128)S(1)} copy-done((f32[1152,576]{0,1:T(8,128)S(1)}, f32[1152,576]{0,1:T(8,128)}, u32[]{:S(2)}) %copy-start) | copy-done | bytes 2654232
  2.4 0.0 copy-start.4
  2.4 1.5 %copy-done.4 = bf16[768,1152]{1,0:T(8,128)(2,1)S(1)} copy-done((bf16[768,1152]{1,0:T(8,128)(2,1)S(1)}, bf16[768,1152]{1,0:T(8,128)(2,1)}, u32[]{:S(2)}) %copy-start.4) | copy-done | bytes 1769496
  3.9 0.0 copy-start.1
  3.9 0.0 copy-start.2
  3.9 0.0 copy-start.3
  3.9 122.3 %shard_map.67 = (f32[576,1152]{1,0:T(8,128)S(1)}, f32[8,128]{1,0:T(8,128)S(1)}) custom-call(bf16[768,1152]{1,0:T(8,128)(2,1)S(1)} %copy-done.4, f32[576,1152]{1,0:T(8,128)S(1)} %bitcast.6, f32[576,1152]{1,0:T(8,128)} %bitcast.8), custom_call_target="tpu_custom_call" | custom-call | flops 16307453952 | bytes 16777216 | tf_op jit(solution)/shard_map/pallas_call | solution.py:358
  126.2 0.0 copy-done.1
  126.2 0.0 copy-done.2
  126.2 0.0 copy-done.3
  126.2 3.5 %shard_map.68 = (f32[576,1152]{1,0:T(8,128)}, f32[576,1152]{1,0:T(8,128)}, f32[576,1152]{1,0:T(8,128)}) custom-call(f32[8,128]{1,0:T(8,128)S(1)} %get-tuple-element.8.sums_ref, f32[576,1152]{1,0:T(8,128)S(1)} %get-tuple-element.9.curved_ref, f32[576,1152]{1,0:T(8,128)S(1)} %bitcast.10, f32[576,1152]{1,0:T(8,128)S(1)} %bitcast.7, f32[576,1152]{1,0:T(8,128)S(1)} %bitcast.9), custom_call_target="tpu_custom_call" | custom-call | tf_op jit(solution)/shard_map/pallas_call | solution.py:422
Async XLA Ops:
  0.6 1.8 %copy-start = (f32[1152,576]{0,1:T(8,128)S(1)}, f32[1152,576]{0,1:T(8,128)}, u32[]{:S(2)}) copy-start(f32[1152,576]{0,1:T(8,128)} %param.6) | copy-start | bytes 7962628
  2.4 1.5 %copy-start.4 = (bf16[768,1152]{1,0:T(8,128)(2,1)S(1)}, bf16[768,1152]{1,0:T(8,128)(2,1)}, u32[]{:S(2)}) copy-start(bf16[768,1152]{1,0:T(8,128)(2,1)} %acts_ref.1) | copy-start | bytes 5308420
  3.9 122.3 %copy-start.1 = (f32[1152,576]{0,1:T(8,128)S(1)}, f32[1152,576]{0,1:T(8,128)}, u32[]{:S(2)}) copy-start(f32[1152,576]{0,1:T(8,128)} %param.6) | copy-start | bytes 7962628
  3.9 122.3 %copy-start.2 = (f32[1152,576]{0,1:T(8,128)S(1)}, f32[1152,576]{0,1:T(8,128)}, u32[]{:S(2)}) copy-start(f32[1152,576]{0,1:T(8,128)} %param.7) | copy-start | bytes 7962628
  3.9 122.3 %copy-start.3 = (f32[1152,576]{0,1:T(8,128)S(1)}, f32[1152,576]{0,1:T(8,128)}, u32[]{:S(2)}) copy-start(f32[1152,576]{0,1:T(8,128)} %param.5) | copy-start | bytes 7962628

commit v4 on v3

--- a/solution.py
+++ b/solution.py
@@ -9,21 +9,20 @@
 PIECES = 3
 CHUNKS = 2 * RING * PIECES
 PAIRS = CHUNKS // 2
-HOP = 3
-SEND_AT = (6, 12)
-LAG = [0, 1, 1 + HOP, 1 + 2 * HOP, 1 + 3 * HOP, 1 + 4 * HOP, 1 + 5 * HOP, 1 + 6 * HOP]
-REST = 6
-STEPS = CHUNKS + REST + LAG[-1]
+SENDS = ((1, 0, 0), (11, 1, 1), (13, 1, 0), (14, 2, 1), (25, 2, 0))
+LAG = (1, 5, 9, 12, 16, 23, 29)
+RESTS = ((6, 7), (10, 9), (14, 1), (18, 2))
+STEPS = CHUNKS + sum(rest for _, rest in RESTS) + LAG[-1]
 MESH = pl.DeviceIdType.MESH
 
 
-def chunk_place(k):
-    late = (k + 18) // 24
-    last = (k + 6) // 24
+def chunk_place(k, turn):
+    late, last = lax.div(k + 18, 24), lax.div(k + 6, 24)
     mid = late - last
-    away = mid * (1 + 2 * (k % 2)) + last * 2
-    other = (1 - late) * (k // 3) + mid * ((k // 2 + 1) % 2) + last * (k % 2)
-    piece = (1 - late) * (k % 3) + mid * ((k + 2) // 4 - 2) + last * (k // 2 - 9)
+    away = mid * (2 + turn * (1 - 2 * (lax.rem(lax.div(lax.rem(k + 3, 4), 2), 2)))) + last * 2
+    other = (1 - late) * lax.div(k, 3) + (mid + last) * lax.rem(k, 2)
+    piece = (1 - late) * lax.rem(k, 3) + mid * (lax.div(k + 2, 4) - 2)
+    piece += last * (lax.div(k, 2) - 9)
     return away, other, piece
 
 
@@ -50,16 +49,30 @@
     def along_y(d):
         return (((y + d + RING) % RING) * 2 + c, mp)
 
-    def first(d):
-        return (dp, ((z + d * c + RING) % RING) * RING + (x + d * (1 - c) + RING) % RING)
-
-    def second(d):
-        return (dp, ((z + d * (1 - c)) % RING) * RING + (x + d * c) % RING)
+    def plane(to_x, to_z):
+        return lax.rem(z + to_z + RING, RING) * RING + lax.rem(x + to_x + RING, RING)
+
+    up, down = plane(1 - c, c), plane(c - 1, -c)
+    second = [plane(o * c, o * (1 - c)) for o in range(RING)]
+    up_slot, down_slot, far_slot = (lax.rem(p1 + o, RING) for o in (1, 3, 2))
+    second_slot = [lax.rem(p2 + o, RING) for o in range(RING)]
+
+    def ahead(k):
+        return up + (down - up) * lax.rem(k, 2)
+
+    def behind(k):
+        return down + (up - down) * lax.rem(k, 2)
+
+    def ahead_slot(k):
+        return up_slot + (down_slot - up_slot) * lax.rem(k, 2)
+
+    def behind_slot(k):
+        return down_slot + (up_slot - down_slot) * lax.rem(k, 2)
 
     sibling = (y * 2 + 1 - c, mp)
 
     def act_rows(away, other, piece):
-        who = ((y + away) % RING) * 2 + (c + other) % 2
+        who = lax.rem(y + away, RING) * 2 + lax.rem(c + other, 2)
         return pl.ds(pl.multiple_of(who * block + piece * rows, rows), rows)
 
     def remote(src, dst, send, recv, to):
@@ -91,7 +104,6 @@
 
     load_dir.wait()
     low[...] = dir_here[...].astype(jnp.bfloat16)
-    curved_ref[...] = jnp.zeros_like(curved_ref)
     pl.semaphore_wait(barrier, 22)
 
     def y_copy(j, way):
@@ -111,10 +123,10 @@
 
     for j in range(PIECES):
         own_copy(j).wait()
+        if j == 0:
+            y_copy(j, 1 - c).start()
         sib_copy(0, j).start()
-        if j == 0:
-            y_copy(j, 0).start()
-            y_copy(j, 1).start()
+    curved_ref[...] = jnp.zeros_like(curved_ref)
 
     def slot_rows(slot):
         return pl.ds(pl.multiple_of(slot * big, 16), big)
@@ -122,44 +134,40 @@
     def lane(slot):
         return pl.ds(pl.multiple_of(slot * lanes, lanes), lanes)
 
-    def way_of(k):
-        return 1 - 2 * (k % 2)
-
     def r1_copy(k, which):
-        s = way_of(k)
+        done = sent.at[lax.div(k, 2)]
         if which == 0:
-            src = part.at[k, slot_rows((p1 + 2) % RING)]
-            return remote(src, pass1.at[k], sent.at[k // 2], r1_recv.at[k, 0], first(s))
-        src = part.at[k, slot_rows((p1 + RING - s) % RING)]
-        return remote(src, got1b.at[k], sent.at[k // 2], r1_recv.at[k, 1], first(-s))
+            src = part.at[k, slot_rows(far_slot)]
+            return remote(src, pass1.at[k], done, r1_recv.at[k, 0], (dp, ahead(k)))
+        src = part.at[k, slot_rows(behind_slot(k))]
+        return remote(src, got1b.at[k], done, r1_recv.at[k, 1], (dp, behind(k)))
 
     def f1_copy(k):
-        s = way_of(k)
-        src = part.at[k, slot_rows((p1 + RING + s) % RING)]
-        return remote(src, got1a.at[k], sent.at[k // 2], f1_recv.at[k], first(s))
+        src = part.at[k, slot_rows(ahead_slot(k))]
+        return remote(src, got1a.at[k], sent.at[lax.div(k, 2)], f1_recv.at[k], (dp, ahead(k)))
 
     def r2_copy(m, o):
-        src = quad.at[m, :, lane((p2 + o) % RING)]
-        return remote(src, got2.at[m, o - 1], sent.at[m], r2_recv.at[m], second(o))
+        src = quad.at[m, :, lane(second_slot[o])]
+        return remote(src, got2.at[m, o - 1], sent.at[m], r2_recv.at[m], (dp, second[o]))
 
     def g1_copy(m, o):
         here = tan.at[m, slot_rows(p1), lane(p2)]
-        return remote(here, here, sent.at[m], g1_recv.at[m], second(o))
+        return remote(here, here, sent.at[m], g1_recv.at[m], (dp, second[o]))
 
     def g2_copy(m, way, whose):
         here = tan.at[m, slot_rows(whose)]
-        to = first(way_of(m) * (1 - 2 * way))
-        return remote(here, here, sent.at[m], g2_recv.at[m, way], to)
+        to = behind(m) if way else ahead(m)
+        return remote(here, here, sent.at[m], g2_recv.at[m, way], (dp, to))
 
     def f2_copy(m, whose):
         here = tan.at[m, slot_rows(whose)]
-        return remote(here, here, sent.at[m], f2_recv.at[m], first(way_of(m)))
+        return remote(here, here, sent.at[m], f2_recv.at[m], (dp, ahead(m)))
 
     def wait_all(sem, some):
         pltpu.make_async_copy(some, some, sem).wait()
 
     def arrive(k):
-        away, other, piece = chunk_place(k)
+        away, other, piece = chunk_place(k, turn)
 
         @pl.when((other == 0) & (away != 0))
         def _():
@@ -182,7 +190,7 @@
 
     def forward_product(k):
         product = lax.dot_general(
-            low[...], acts[act_rows(*chunk_place(k)), :], (((1,), (1,)), ((), ())),
+            low[...], acts[act_rows(*chunk_place(k, turn)), :], (((1,), (1,)), ((), ())),
             preferred_element_type=jnp.float32,
         )
         part[k] = product.astype(jnp.bfloat16)
@@ -191,7 +199,7 @@
 
     def pass_on(k):
         r1_copy(k, 0).wait_recv()
-        here = slot_rows((p1 + RING + way_of(k)) % RING)
+        here = slot_rows(ahead_slot(k))
         part[k, here, :] = (
             part[k, here, :].astype(jnp.float32) + pass1[k].astype(jnp.float32)
         ).astype(jnp.bfloat16)
@@ -200,17 +208,18 @@
     def quarter(k):
         f1_copy(k).wait_recv()
         r1_copy(k, 1).wait_recv()
-        half = pl.ds(pl.multiple_of((k % 2) * rows, rows), rows)
-        quad[k // 2, :, half] = (
+        m, odd = lax.div(k, 2), lax.rem(k, 2)
+        half = pl.ds(pl.multiple_of(odd * rows, rows), rows)
+        quad[m, :, half] = (
             part[k, slot_rows(p1), :].astype(jnp.float32)
             + got1a[k].astype(jnp.float32)
             + got1b[k].astype(jnp.float32)
         ).astype(jnp.bfloat16)
 
-        @pl.when(k % 2 == 1)
+        @pl.when(odd == 1)
         def _():
             for o in range(1, RING):
-                r2_copy(k // 2, o).start()
+                r2_copy(m, o).start()
 
     def total(m):
         wait_all(r2_recv.at[m], got2.at[m])
@@ -227,22 +236,22 @@
         g2_copy(m, 1, p1).start()
 
     def spread_on(m):
-        whose = (p1 + RING - way_of(m)) % RING
+        whose = behind_slot(m)
         g2_copy(m, 0, whose).wait_recv()
         f2_copy(m, whose).start()
 
     def back_product(m):
-        g2_copy(m, 1, (p1 + RING + way_of(m)) % RING).wait_recv()
-        f2_copy(m, (p1 + 2) % RING).wait_recv()
+        g2_copy(m, 1, ahead_slot(m)).wait_recv()
+        f2_copy(m, far_slot).wait_recv()
 
         @pl.loop(0, acts.shape[1] // WIDE)
         def _(h):
             at = pl.ds(pl.multiple_of(h * WIDE, WIDE), WIDE)
             curved_ref[:, at] += jnp.dot(
-                tan[m, :, 0:rows], acts[act_rows(*chunk_place(2 * m)), at],
+                tan[m, :, 0:rows], acts[act_rows(*chunk_place(2 * m, turn)), at],
                 preferred_element_type=jnp.float32,
             ) + jnp.dot(
-                tan[m, :, rows : 2 * rows], acts[act_rows(*chunk_place(2 * m + 1)), at],
+                tan[m, :, rows : 2 * rows], acts[act_rows(*chunk_place(2 * m + 1, turn)), at],
                 preferred_element_type=jnp.float32,
             )
 
@@ -253,30 +262,33 @@
         wait_all(sent.at[m], tan.at[m, pl.ds(0, 3 * big)])
 
     stages = [
-        (2, pass_on, 1), (3, quarter, 1), (4, total, 2), (5, spread, 2), (6, spread_on, 2),
-        (0, arrive, 1), (1, forward_product, 1), (7, back_product, 2),
+        (LAG[5], spread_on, 2), (LAG[4], spread, 2), (LAG[3], total, 2), (LAG[2], quarter, 1),
+        (LAG[1], pass_on, 1), (LAG[0], arrive, 1), (LAG[0], forward_product, 1),
+        (LAG[6], back_product, 2),
     ]
 
     @pl.loop(0, STEPS)
     def _(step):
-        for j, at in ((1, SEND_AT[0]), (2, SEND_AT[1])):
+        for at, j, way in SENDS:
 
             @pl.when(step == at)
-            def _(j=j):
-                y_copy(j, 0).start()
-                y_copy(j, 1).start()
-
-        for at, stage, every in stages:
-            turn_of = step - LAG[at]
-            rested = (turn_of + 64 - 2 * PIECES - REST) // 64
-            k = turn_of - rested * REST
-
-            @pl.when(
-                (k >= 0) & (k < CHUNKS) & ((rested == 1) | (k < 2 * PIECES))
-                & (k % every == every - 1)
-            )
+            def _(j=j, way=way):
+                y_copy(j, (way + c) % 2).start()
+
+        for lag, stage, every in stages:
+            turn_of = step - lag
+            k, go, begin = turn_of, turn_of >= 0, 0
+            for at, rest in RESTS:
+                go &= (turn_of < at + begin) | (turn_of >= at + begin + rest)
+                begin += rest
+                k = jnp.where(turn_of >= at + begin, turn_of - begin, k)
+            go &= turn_of < CHUNKS + begin
+            if every == 2:
+                go &= lax.rem(k, 2) == 1
+
+            @pl.when(go)
             def _(k=k, stage=stage, every=every):
-                stage(k // every)
+                stage(lax.div(k, every))
 
     for j in range(PIECES):
         y_copy(j, 0).wait_send()
@@ -383,7 +395,7 @@
             dma((24,)), dma((24,)),
         ],
         compiler_params=pltpu.CompilerParams(
-            collective_id=0, has_side_effects=True, vmem_limit_bytes=46 * 2**20
+            collective_id=0, has_side_effects=True, vmem_limit_bytes=53 * 2**20
         ),
         cost_estimate=pl.CostEstimate(
             flops=32 * block * hidden * columns, bytes_accessed=16 * 2**20, transcendentals=0

time: 130 us -> 124 us (0.954)
  Pallas kernels: 126 us -> 122 us
  local copies, waits for them, and re-layouts: 3.23 us -> 1.76 us
    pallas_call x1, Pallas kernels: 122 us -> 118 us  [curvature(): pl.pallas_call(kernel, out_shape=(jax.ShapeDtypeStruct((columns, hidden),...]
    unnamed x10 -> x8, local copies, waits for them, and re-layouts: 3.23 us -> 1.76 us
where the time goes in v4:
time: 124 us
  Pallas kernels  122 us (98%)
  local copies, waits for them, and re-layouts  1.76 us (1%)
    pallas_call x1, Pallas kernels, curvature(): pl.pallas_call(kernel, out_shape=(jax.ShapeDtypeStruct((columns, hidden),...  118 us
    pallas_call x1, Pallas kernels, finish(): pl.pallas_call(finish_kernel, out_shape=(field,) * 3, in_specs=[vmem] * 5...  3.49 us

profile of v4, /device:TPU:1, one launch (start us, length us, event | category | flops | bytes accessed | tf_op | source)
XLA Modules:
  0.0 124.1 jit_solution(8623124164831302381)
XLA Ops:
  0.6 0.0 copy-start
  0.6 0.0 copy-start.1
  0.7 0.0 copy-start.2
  0.7 118.2 %shard_map.67 = (f32[576,1152]{1,0:T(8,128)}, f32[8,128]{1,0:T(8,128)S(1)}) custom-call(bf16[768,1152]{1,0:T(8,128)(2,1)} %acts_ref.1, f32[576,1152]{1,0:T(8,128)} %bitcast.6, f32[576,1152]{1,0:T(8,128)} %bitcast.8), custom_call_target="tpu_custom_call" | custom-call | flops 16307453952 | bytes 16777216 | tf_op jit(solution)/shard_map/pallas_call | solution.py:370
  118.9 0.0 copy-done
  118.9 0.0 copy-done.1
  118.9 0.0 copy-done.2
  118.9 0.0 copy-start.3
  118.9 1.7 %copy-done.3 = f32[576,1152]{1,0:T(8,128)S(1)} copy-done((f32[576,1152]{1,0:T(8,128)S(1)}, f32[576,1152]{1,0:T(8,128)}, u32[]{:S(2)}) %copy-start.3) | copy-done | bytes 2654232
  120.6 3.5 %shard_map.68 = (f32[576,1152]{1,0:T(8,128)}, f32[576,1152]{1,0:T(8,128)}, f32[576,1152]{1,0:T(8,128)}) custom-call(f32[8,128]{1,0:T(8,128)S(1)} %get-tuple-element.8.sums_ref, f32[576,1152]{1,0:T(8,128)S(1)} %copy-done.3, f32[576,1152]{1,0:T(8,128)S(1)} %bitcast.10, f32[576,1152]{1,0:T(8,128)S(1)} %bitcast.7, f32[576,1152]{1,0:T(8,128)S(1)} %bitcast.9), custom_call_target="tpu_custom_call" | custom-call | tf_op jit(solution)/shard_map/pallas_call | solution.py:434
Async XLA Ops:
  0.6 118.2 %copy-start = (f32[1152,576]{0,1:T(8,128)S(1)}, f32[1152,576]{0,1:T(8,128)}, u32[]{:S(2)}) copy-start(f32[1152,576]{0,1:T(8,128)} %param.6) | copy-start | bytes 7962628
  0.6 118.2 %copy-start.1 = (f32[1152,576]{0,1:T(8,128)S(1)}, f32[1152,576]{0,1:T(8,128)}, u32[]{:S(2)}) copy-start(f32[1152,576]{0,1:T(8,128)} %param.7) | copy-start | bytes 7962628
  0.7 118.2 %copy-start.2 = (f32[1152,576]{0,1:T(8,128)S(1)}, f32[1152,576]{0,1:T(8,128)}, u32[]{:S(2)}) copy-start(f32[1152,576]{0,1:T(8,128)} %param.5) | copy-start | bytes 7962628
  118.9 1.8 %copy-start.3 = (f32[576,1152]{1,0:T(8,128)S(1)}, f32[576,1152]{1,0:T(8,128)}, u32[]{:S(2)}) copy-start(f32[576,1152]{1,0:T(8,128)} %get-tuple-element.9.curved_ref) | copy-start | bytes 7962628

commit v5 on v4

--- a/solution.py
+++ b/solution.py
@@ -9,9 +9,9 @@
 PIECES = 3
 CHUNKS = 2 * RING * PIECES
 PAIRS = CHUNKS // 2
-SENDS = ((1, 0, 0), (11, 1, 1), (13, 1, 0), (14, 2, 1), (25, 2, 0))
-LAG = (1, 5, 9, 12, 16, 23, 29)
-RESTS = ((6, 7), (10, 9), (14, 1), (18, 2))
+SENDS = ((3, 0, 0), (4, 1, 1), (7, 1, 0), (6, 2, 1), (9, 2, 0))
+LAG = (1, 4, 7, 10, 13, 18, 23)
+RESTS = ((6, 4), (10, 6), (14, 0), (18, 1))
 STEPS = CHUNKS + sum(rest for _, rest in RESTS) + LAG[-1]
 MESH = pl.DeviceIdType.MESH
 
@@ -262,8 +262,8 @@
         wait_all(sent.at[m], tan.at[m, pl.ds(0, 3 * big)])
 
     stages = [
-        (LAG[5], spread_on, 2), (LAG[4], spread, 2), (LAG[3], total, 2), (LAG[2], quarter, 1),
-        (LAG[1], pass_on, 1), (LAG[0], arrive, 1), (LAG[0], forward_product, 1),
+        (LAG[1], pass_on, 1), (LAG[2], quarter, 1), (LAG[3], total, 2), (LAG[4], spread, 2),
+        (LAG[5], spread_on, 2), (LAG[0], arrive, 1), (LAG[0], forward_product, 1),
         (LAG[6], back_product, 2),
     ]
 

time: 124 us -> 122 us (0.984)
  Pallas kernels: 122 us -> 119 us
    pallas_call x1, Pallas kernels: 118 us -> 116 us  [curvature(): pl.pallas_call(kernel, out_shape=(jax.ShapeDtypeStruct((columns, hidden),...]
where the time goes in v5:
time: 122 us
  Pallas kernels  119 us (98%)
  local copies, waits for them, and re-layouts  1.76 us (1%)
    pallas_call x1, Pallas kernels, curvature(): pl.pallas_call(kernel, out_shape=(jax.ShapeDtypeStruct((columns, hidden),...  116 us
    pallas_call x1, Pallas kernels, finish(): pl.pallas_call(finish_kernel, out_shape=(field,) * 3, in_specs=[vmem] * 5...  3.49 us

profile of v5, /device:TPU:1, one launch (start us, length us, event | category | flops | bytes accessed | tf_op | source)
XLA Modules:
  0.0 121.7 jit_solution(2312840094346530302)
XLA Ops:
  0.6 0.0 copy-start
  0.6 0.0 copy-start.1
  0.7 0.0 copy-start.2
  0.7 115.7 %shard_map.67 = (f32[576,1152]{1,0:T(8,128)}, f32[8,128]{1,0:T(8,128)S(1)}) custom-call(bf16[768,1152]{1,0:T(8,128)(2,1)} %acts_ref.1, f32[576,1152]{1,0:T(8,128)} %bitcast.6, f32[576,1152]{1,0:T(8,128)} %bitcast.8), custom_call_target="tpu_custom_call" | custom-call | flops 16307453952 | bytes 16777216 | tf_op jit(solution)/shard_map/pallas_call | solution.py:370
  116.4 0.0 copy-done
  116.4 0.0 copy-done.1
  116.4 0.0 copy-done.2
  116.4 0.0 copy-start.3
  116.4 1.7 %copy-done.3 = f32[576,1152]{1,0:T(8,128)S(1)} copy-done((f32[576,1152]{1,0:T(8,128)S(1)}, f32[576,1152]{1,0:T(8,128)}, u32[]{:S(2)}) %copy-start.3) | copy-done | bytes 2654232
  118.2 3.5 %shard_map.68 = (f32[576,1152]{1,0:T(8,128)}, f32[576,1152]{1,0:T(8,128)}, f32[576,1152]{1,0:T(8,128)}) custom-call(f32[8,128]{1,0:T(8,128)S(1)} %get-tuple-element.8.sums_ref, f32[576,1152]{1,0:T(8,128)S(1)} %copy-done.3, f32[576,1152]{1,0:T(8,128)S(1)} %bitcast.10, f32[576,1152]{1,0:T(8,128)S(1)} %bitcast.7, f32[576,1152]{1,0:T(8,128)S(1)} %bitcast.9), custom_call_target="tpu_custom_call" | custom-call | tf_op jit(solution)/shard_map/pallas_call | solution.py:434
Async XLA Ops:
  0.6 115.8 %copy-start = (f32[1152,576]{0,1:T(8,128)S(1)}, f32[1152,576]{0,1:T(8,128)}, u32[]{:S(2)}) copy-start(f32[1152,576]{0,1:T(8,128)} %param.6) | copy-start | bytes 7962628
  0.6 115.8 %copy-start.1 = (f32[1152,576]{0,1:T(8,128)S(1)}, f32[1152,576]{0,1:T(8,128)}, u32[]{:S(2)}) copy-start(f32[1152,576]{0,1:T(8,128)} %param.7) | copy-start | bytes 7962628
  0.7 115.8 %copy-start.2 = (f32[1152,576]{0,1:T(8,128)S(1)}, f32[1152,576]{0,1:T(8,128)}, u32[]{:S(2)}) copy-start(f32[1152,576]{0,1:T(8,128)} %param.5) | copy-start | bytes 7962628
  116.4 1.8 %copy-start.3 = (f32[576,1152]{1,0:T(8,128)S(1)}, f32[576,1152]{1,0:T(8,128)}, u32[]{:S(2)}) copy-start(f32[576,1152]{1,0:T(8,128)} %get-tuple-element.9.curved_ref) | copy-start | bytes 7962628

commit v6 on v5

--- a/solution.py
+++ b/solution.py
@@ -138,9 +138,9 @@
         done = sent.at[lax.div(k, 2)]
         if which == 0:
             src = part.at[k, slot_rows(far_slot)]
-            return remote(src, pass1.at[k], done, r1_recv.at[k, 0], (dp, ahead(k)))
+            return remote(src, pass1.at[k], done, r1_recv.at[k], (dp, ahead(k)))
         src = part.at[k, slot_rows(behind_slot(k))]
-        return remote(src, got1b.at[k], done, r1_recv.at[k, 1], (dp, behind(k)))
+        return remote(src, got1b.at[k], done, f1_recv.at[k], (dp, behind(k)))
 
     def f1_copy(k):
         src = part.at[k, slot_rows(ahead_slot(k))]
@@ -157,7 +157,8 @@
     def g2_copy(m, way, whose):
         here = tan.at[m, slot_rows(whose)]
         to = behind(m) if way else ahead(m)
-        return remote(here, here, sent.at[m], g2_recv.at[m, way], (dp, to))
+        came = f2_recv.at[m] if way else g2_recv.at[m]
+        return remote(here, here, sent.at[m], came, (dp, to))
 
     def f2_copy(m, whose):
         here = tan.at[m, slot_rows(whose)]
@@ -206,8 +207,7 @@
         f1_copy(k).start()
 
     def quarter(k):
-        f1_copy(k).wait_recv()
-        r1_copy(k, 1).wait_recv()
+        wait_all(f1_recv.at[k], part.at[k, pl.ds(0, 2 * big)])
         m, odd = lax.div(k, 2), lax.rem(k, 2)
         half = pl.ds(pl.multiple_of(odd * rows, rows), rows)
         quad[m, :, half] = (
@@ -241,8 +241,7 @@
         f2_copy(m, whose).start()
 
     def back_product(m):
-        g2_copy(m, 1, ahead_slot(m)).wait_recv()
-        f2_copy(m, far_slot).wait_recv()
+        wait_all(f2_recv.at[m], tan.at[m, pl.ds(0, 2 * big)])
 
         @pl.loop(0, acts.shape[1] // WIDE)
         def _(h):
@@ -290,13 +289,6 @@
             def _(k=k, stage=stage, every=every):
                 stage(lax.div(k, every))
 
-    for j in range(PIECES):
-        y_copy(j, 0).wait_send()
-        y_copy(j, 1).wait_send()
-        fwd_copy(j).wait_send()
-        for away in range(RING):
-            sib_copy(away, j).wait_send()
-
     load_res.wait()
     direction, residual = dir_here[...], res_here[...]
     curved = curved_ref[...] / tokens + 1.0 * direction
@@ -315,19 +307,24 @@
 
     def plane_copy(o, whose):
         here = tiles.at[whose]
-        return remote(here, here, sum_send.at[o], sum_recv.at[o], (dp, (mp + o) % 16))
+        return remote(here, here, sum_send.at[0], sum_recv.at[0], (dp, (mp + o) % 16))
 
     def column_copy(o, whose):
         here = tiles.at[16 + whose]
-        return remote(here, here, sum_send.at[16 + o], sum_recv.at[16 + o], ((dp + o) % 8, mp))
+        return remote(here, here, sum_send.at[1], sum_recv.at[1], ((dp + o) % 8, mp))
 
     @pl.loop(1, 16)
     def _(o):
         plane_copy(o, mp).start()
 
-    @pl.loop(1, 16)
-    def _(o):
-        plane_copy(o, (mp + 16 - o) % 16).wait_recv()
+    for j in range(PIECES):
+        y_copy(j, 0).wait_send()
+        y_copy(j, 1).wait_send()
+        fwd_copy(j).wait_send()
+        for away in range(RING):
+            sib_copy(away, j).wait_send()
+
+    wait_all(sum_recv.at[0], tiles.at[pl.ds(0, 15)])
 
     subtotal = tiles[0]
     for i in range(1, 16):
@@ -338,22 +335,15 @@
     def _(o):
         column_copy(o, dp).start()
 
-    @pl.loop(1, 8)
-    def _(o):
-        column_copy(o, (dp + 8 - o) % 8).wait_recv()
+    wait_all(sum_recv.at[1], tiles.at[pl.ds(0, 7)])
 
     whole = tiles[16]
     for i in range(1, 8):
         whole = whole + tiles[16 + i]
     sums_ref[...] = jnp.broadcast_to(whole, (8, 128))
 
-    @pl.loop(1, 16)
-    def _(o):
-        plane_copy(o, mp).wait_send()
-
-    @pl.loop(1, 8)
-    def _(o):
-        column_copy(o, dp).wait_send()
+    wait_all(sum_send.at[0], tiles.at[pl.ds(0, 15)])
+    wait_all(sum_send.at[1], tiles.at[pl.ds(0, 7)])
 
 
 WIDE = 384
@@ -390,9 +380,9 @@
             pltpu.VMEM((columns, hidden), f32),
             dma((PIECES + 2,)), dma((2, PIECES)), dma((RING, PIECES)), dma((PIECES,)),
             dma((RING, PIECES)), dma((RING, PIECES)),
-            dma((PAIRS,)), dma((CHUNKS, 2)), dma((CHUNKS,)), dma((PAIRS,)), dma((PAIRS,)),
-            dma((PAIRS, 2)), dma((PAIRS,)),
-            dma((24,)), dma((24,)),
+            dma((PAIRS,)), dma((CHUNKS,)), dma((CHUNKS,)), dma((PAIRS,)), dma((PAIRS,)),
+            dma((PAIRS,)), dma((PAIRS,)),
+            dma((2,)), dma((2,)),
         ],
         compiler_params=pltpu.CompilerParams(
             collective_id=0, has_side_effects=True, vmem_limit_bytes=53 * 2**20

time: 122 us -> 121 us (level)
  no operation moved by 1% of the time
where the time goes in v6:
time: 121 us
  Pallas kernels  118 us (98%)
  local copies, waits for them, and re-layouts  1.76 us (1%)
    pallas_call x1, Pallas kernels, curvature(): pl.pallas_call(kernel, out_shape=(jax.ShapeDtypeStruct((columns, hidden),...  115 us
    pallas_call x1, Pallas kernels, finish(): pl.pallas_call(finish_kernel, out_shape=(field,) * 3, in_specs=[vmem] * 5...  3.49 us

profile of v6, /device:TPU:1, one launch (start us, length us, event | category | flops | bytes accessed | tf_op | source)
XLA Modules:
  0.0 120.8 jit_solution(6859141162069361012)
XLA Ops:
  0.6 0.0 copy-start
  0.6 0.0 copy-start.1
  0.7 0.0 copy-start.2
  0.7 114.9 %shard_map.67 = (f32[576,1152]{1,0:T(8,128)}, f32[8,128]{1,0:T(8,128)S(1)}) custom-call(bf16[768,1152]{1,0:T(8,128)(2,1)} %acts_ref.1, f32[576,1152]{1,0:T(8,128)} %bitcast.6, f32[576,1152]{1,0:T(8,128)} %bitcast.8), custom_call_target="tpu_custom_call" | custom-call | flops 16307453952 | bytes 16777216 | tf_op jit(solution)/shard_map/pallas_call | solution.py:360
  115.6 0.0 copy-done
  115.6 0.0 copy-done.1
  115.6 0.0 copy-done.2
  115.6 0.0 copy-start.3
  115.6 1.7 %copy-done.3 = f32[576,1152]{1,0:T(8,128)S(1)} copy-done((f32[576,1152]{1,0:T(8,128)S(1)}, f32[576,1152]{1,0:T(8,128)}, u32[]{:S(2)}) %copy-start.3) | copy-done | bytes 2654232
  117.3 3.5 %shard_map.68 = (f32[576,1152]{1,0:T(8,128)}, f32[576,1152]{1,0:T(8,128)}, f32[576,1152]{1,0:T(8,128)}) custom-call(f32[8,128]{1,0:T(8,128)S(1)} %get-tuple-element.8.sums_ref, f32[576,1152]{1,0:T(8,128)S(1)} %copy-done.3, f32[576,1152]{1,0:T(8,128)S(1)} %bitcast.10, f32[576,1152]{1,0:T(8,128)S(1)} %bitcast.7, f32[576,1152]{1,0:T(8,128)S(1)} %bitcast.9), custom_call_target="tpu_custom_call" | custom-call | tf_op jit(solution)/shard_map/pallas_call | solution.py:424
Async XLA Ops:
  0.6 114.9 %copy-start = (f32[1152,576]{0,1:T(8,128)S(1)}, f32[1152,576]{0,1:T(8,128)}, u32[]{:S(2)}) copy-start(f32[1152,576]{0,1:T(8,128)} %param.6) | copy-start | bytes 7962628
  0.6 114.9 %copy-start.1 = (f32[1152,576]{0,1:T(8,128)S(1)}, f32[1152,576]{0,1:T(8,128)}, u32[]{:S(2)}) copy-start(f32[1152,576]{0,1:T(8,128)} %param.7) | copy-start | bytes 7962628
  0.7 114.9 %copy-start.2 = (f32[1152,576]{0,1:T(8,128)S(1)}, f32[1152,576]{0,1:T(8,128)}, u32[]{:S(2)}) copy-start(f32[1152,576]{0,1:T(8,128)} %param.5) | copy-start | bytes 7962628
  115.6 1.8 %copy-start.3 = (f32[576,1152]{1,0:T(8,128)S(1)}, f32[576,1152]{1,0:T(8,128)}, u32[]{:S(2)}) copy-start(f32[576,1152]{1,0:T(8,128)} %get-tuple-element.9.curved_ref) | copy-start | bytes 7962628

commit v7 on v6

--- a/solution.py
+++ b/solution.py
@@ -10,8 +10,8 @@
 CHUNKS = 2 * RING * PIECES
 PAIRS = CHUNKS // 2
 SENDS = ((3, 0, 0), (4, 1, 1), (7, 1, 0), (6, 2, 1), (9, 2, 0))
-LAG = (1, 4, 7, 10, 13, 18, 23)
-RESTS = ((6, 4), (10, 6), (14, 0), (18, 1))
+LAG = (1, 4, 7, 9, 12, 17, 22)
+RESTS = ((6, 4), (10, 6))
 STEPS = CHUNKS + sum(rest for _, rest in RESTS) + LAG[-1]
 MESH = pl.DeviceIdType.MESH
 

time: 121 us -> 121 us (level)
  no operation moved by 1% of the time
where the time goes in v7:
time: 121 us
  Pallas kernels  118 us (98%)
  local copies, waits for them, and re-layouts  1.76 us (1%)
    pallas_call x1, Pallas kernels, curvature(): pl.pallas_call(kernel, out_shape=(jax.ShapeDtypeStruct((columns, hidden),...  115 us
    pallas_call x1, Pallas kernels, finish(): pl.pallas_call(finish_kernel, out_shape=(field,) * 3, in_specs=[vmem] * 5...  3.49 us

profile of v7, /device:TPU:1, one launch (start us, length us, event | category | flops | bytes accessed | tf_op | source)
XLA Modules:
  0.0 120.8 jit_solution(14915331003949680766)
XLA Ops:
  0.6 0.0 copy-start
  0.6 0.0 copy-start.1
  0.7 0.0 copy-start.2
  0.7 114.9 %shard_map.67 = (f32[576,1152]{1,0:T(8,128)}, f32[8,128]{1,0:T(8,128)S(1)}) custom-call(bf16[768,1152]{1,0:T(8,128)(2,1)} %acts_ref.1, f32[576,1152]{1,0:T(8,128)} %bitcast.6, f32[576,1152]{1,0:T(8,128)} %bitcast.8), custom_call_target="tpu_custom_call" | custom-call | flops 16307453952 | bytes 16777216 | tf_op jit(solution)/shard_map/pallas_call | solution.py:360
  115.5 0.0 copy-done
  115.6 0.0 copy-done.1
  115.6 0.0 copy-done.2
  115.6 0.0 copy-start.3
  115.6 1.7 %copy-done.3 = f32[576,1152]{1,0:T(8,128)S(1)} copy-done((f32[576,1152]{1,0:T(8,128)S(1)}, f32[576,1152]{1,0:T(8,128)}, u32[]{:S(2)}) %copy-start.3) | copy-done | bytes 2654232
  117.3 3.5 %shard_map.68 = (f32[576,1152]{1,0:T(8,128)}, f32[576,1152]{1,0:T(8,128)}, f32[576,1152]{1,0:T(8,128)}) custom-call(f32[8,128]{1,0:T(8,128)S(1)} %get-tuple-element.8.sums_ref, f32[576,1152]{1,0:T(8,128)S(1)} %copy-done.3, f32[576,1152]{1,0:T(8,128)S(1)} %bitcast.10, f32[576,1152]{1,0:T(8,128)S(1)} %bitcast.7, f32[576,1152]{1,0:T(8,128)S(1)} %bitcast.9), custom_call_target="tpu_custom_call" | custom-call | tf_op jit(solution)/shard_map/pallas_call | solution.py:424
Async XLA Ops:
  0.6 114.9 %copy-start = (f32[1152,576]{0,1:T(8,128)S(1)}, f32[1152,576]{0,1:T(8,128)}, u32[]{:S(2)}) copy-start(f32[1152,576]{0,1:T(8,128)} %param.6) | copy-start | bytes 7962628
  0.6 114.9 %copy-start.1 = (f32[1152,576]{0,1:T(8,128)S(1)}, f32[1152,576]{0,1:T(8,128)}, u32[]{:S(2)}) copy-start(f32[1152,576]{0,1:T(8,128)} %param.7) | copy-start | bytes 7962628
  0.7 114.9 %copy-start.2 = (f32[1152,576]{0,1:T(8,128)S(1)}, f32[1152,576]{0,1:T(8,128)}, u32[]{:S(2)}) copy-start(f32[1152,576]{0,1:T(8,128)} %param.5) | copy-start | bytes 7962628
  115.6 1.8 %copy-start.3 = (f32[576,1152]{1,0:T(8,128)S(1)}, f32[576,1152]{1,0:T(8,128)}, u32[]{:S(2)}) copy-start(f32[576,1152]{1,0:T(8,128)} %get-tuple-element.9.curved_ref) | copy-start | bytes 7962628
